TPU v7x, 512 devices: a whole 4x4x16 slice. The times are simulated.
512 devices in a mesh: shot: 64 (over z_lo, y, x), off: 8 (over z_hi, core).
Axes of the slice: x: 4, y: 4, z: 16 (z_hi: 4, z_lo: 4; z = z_hi * 4 + z_lo), core: 2. Of those that a mesh axis runs over, the one named last changes fastest.
Arguments:
- earth_model: float32 [4096, 40], P('shot'), may hold values from -3 to 3
- layer_count: int32 [4096], P('shot'), may hold values from 20 to 40, as said below
- thickness: float32 [40], replicated, may hold values from 0.005 to 0.04
- frequency: float32 [5], replicated, may hold values from 0.5 to 4
- midpoint_shift: int32 [64], replicated, may hold values from 0 to 64, as said below
- filters: bfloat16 [201, 64], P(None, 'off'), may hold values from -0.4375 to 0.4375
- weights: bfloat16 [5, 64, 4096], P(None, 'off', 'shot'), may hold values from 0.019897461 to 0.19921875
- residual: bfloat16 [5, 64, 4096], P(None, 'off', 'shot'), may hold values from -6 to 6
Outputs:
- normal: float32 [4096, 1600], P(('shot', 'off'))
- gradient: float32 [4096, 40], P(('shot', 'off'))
Inputs may be any that keep to these rules, and one draw needn't show every extreme that they name: `midpoint_shift`: nondecreasing along the offsets; the last offset's shift is exactly 64. `layer_count`: some midpoint has all 40 layers active.
All inputs are finite; a program needn't handle non-finite values.
Results may differ from a plain program's by a relative error of at most 0.003.
Values may be sent and summed in bfloat16 or wider, within the bound.
A program may use at most 192 MiB of HBM per device.

v0:
```python
import functools

import jax
import jax.numpy as jnp
from jax import lax
from jax.experimental import pallas as pl
from jax.experimental.pallas import tpu as pltpu
from jax.sharding import PartitionSpec as P

MESH = pl.DeviceIdType.MESH
F32 = jnp.float32
BF16 = jnp.bfloat16
LANES = 128
SUB = 8
HALFSPACE = 64.0


def nt_dot(left, right):
    return lax.dot_general(left, right, (((1,), (1,)), ((), ())), preferred_element_type=F32)


def lane_index(rows, lanes=LANES):
    return lax.broadcasted_iota(jnp.int32, (rows, lanes), 1)


def kernel(
    model_ref,
    count_ref,
    thick_ref,
    freq_ref,
    shift_ref,
    filter_ref,
    weight_ref,
    resid_ref,
    normal_ref,
    grad_ref,
    small,
    rows,
    send_a,
    send_b,
    recv_a,
    recv_b,
    sigma_b,
    depth_b,
    part_s,
    part_g,
    sens,
    right,
    send_sem_a,
    send_sem_b,
    recv_sem_a,
    recv_sem_b,
):
    layers = model_ref.shape[0]
    freqs = weight_ref.shape[0]
    taps = filter_ref.shape[1]
    halves = -(-taps // LANES)
    shots = lax.axis_size("shot")
    offs = lax.axis_size("off")
    shot = lax.axis_index("shot")
    off = lax.axis_index("off")
    before = lax.rem(shot + shots - 1, shots)
    after = lax.rem(shot + 1, shots)
    others = [lax.rem(off + step, offs) for step in range(1, offs)]

    barrier = pltpu.get_barrier_semaphore()
    for other in others:
        pl.semaphore_signal(barrier, inc=1, device_id=(shot, other), device_id_type=MESH)
    for other in range(offs):
        pl.semaphore_signal(barrier, inc=1, device_id=(after, other), device_id_type=MESH)

    small[...] = jnp.zeros_like(small)
    block = model_ref.shape[1]
    small[0:layers, 0:block] = model_ref[...]
    small[layers : layers + 1, 0:block] = count_ref[...].astype(F32)
    small[layers + 1 : layers + 2, 0 : shift_ref.shape[1]] = shift_ref[...].astype(F32)
    small[...] = small[...].T
    own = small[pl.ds(pl.multiple_of(off * SUB, SUB), SUB), :]
    shift = own[:, layers + 1 : layers + 2].astype(jnp.int32)
    shift = jnp.broadcast_to(shift, (SUB, LANES))

    rows[...] = jnp.zeros_like(rows)
    bits = [(shift & (1 << b)) != 0 for b in range(7)]
    for q, ref in enumerate((weight_ref, resid_ref)):
        for f in range(freqs):
            x = ref[f].astype(F32)
            x = jnp.concatenate([x, jnp.zeros((SUB, LANES - x.shape[1]), F32)], axis=1)
            for b in range(7):
                x = jnp.where(bits[b], pltpu.roll(x, LANES - (1 << b), 1), x)
            rows[pl.ds(pl.multiple_of((off + f) * SUB, SUB), SUB), q * LANES : (q + 1) * LANES] = x
    by_weight = rows[:, 0:LANES].T
    by_resid = rows[:, LANES : 2 * LANES].T
    columns = filter_ref[...].astype(F32)
    columns = jnp.concatenate([columns, jnp.zeros((SUB, halves * LANES - taps), F32)], axis=1)
    columns = jnp.concatenate([columns[:, h * LANES : (h + 1) * LANES] for h in range(halves)], axis=0)
    columns = columns.astype(BF16)
    has_before = shot > 0
    for j in range(offs):
        at = slice(j * SUB, (j + 1) * SUB)
        send_a[j, 0:16] = jnp.concatenate([by_weight[at], by_resid[at]], axis=0).astype(BF16)
        send_a[j, 16:32] = columns
        at = slice(offs * SUB + j * SUB, offs * SUB + (j + 1) * SUB)
        tile = jnp.concatenate([by_weight[at], by_resid[at]], axis=0)
        send_b[j] = jnp.where(has_before, tile, 0.0).astype(BF16)

    pl.semaphore_wait(barrier, 2 * offs - 1)

    def copy_a(source, slot, device):
        return pltpu.make_async_remote_copy(
            src_ref=send_a.at[source],
            dst_ref=recv_a.at[slot],
            send_sem=send_sem_a.at[source],
            recv_sem=recv_sem_a.at[slot],
            device_id=(shot, device),
            device_id_type=MESH,
        )

    def copy_b(source, slot, device):
        return pltpu.make_async_remote_copy(
            src_ref=send_b.at[source],
            dst_ref=recv_b.at[slot],
            send_sem=send_sem_b.at[source],
            recv_sem=recv_sem_b.at[slot],
            device_id=(before, device),
            device_id_type=MESH,
        )

    for other in others:
        copy_a(other, off, other).start()
    for other in others + [off]:
        copy_b(other, off, other).start()
    recv_a[off] = send_a[off]

    layer = lane_index(SUB)
    count = jnp.broadcast_to(own[:, layers : layers + 1], (SUB, LANES)).astype(jnp.int32)
    thick = jnp.concatenate([thick_ref[...], jnp.zeros((1, LANES - layers), F32)], axis=1)
    thick = jnp.broadcast_to(thick, (SUB, LANES))
    depth = jnp.where(layer < count - 1, thick, jnp.where(layer == count - 1, HALFSPACE, 0.0))
    sigma = jnp.exp(own)
    for i in range(layers):
        sigma_b[i] = jnp.broadcast_to(sigma[:, i : i + 1], (SUB, LANES))
        depth_b[i] = jnp.broadcast_to(depth[:, i : i + 1], (SUB, LANES))
    lam = []
    for h in range(halves):
        tap = jnp.minimum(layer + h * LANES, taps - 1).astype(F32)
        lam.append(jnp.exp(-3.0 + 6.0 * tap / (taps - 1)))
    lam2 = [x * x for x in lam]
    omega = [freq_ref[f] for f in range(freqs)]
    chunks = [(f, h) for f in range(freqs) for h in range(halves)]

    def upward(step, carry):
        i = layers - 1 - step
        sig = sigma_b[i]
        thickness = depth_b[i]
        result = []
        for c, (f, h) in enumerate(chunks):
            num, den = carry[2 * c], carry[2 * c + 1]
            e1 = omega[f] * sig
            a = lam2[h] + e1
            r = lax.rsqrt(a)
            v = a * r
            t = jnp.tanh(v * thickness)
            tr = t * r
            new_num = num + (v * t) * den
            new_den = den + tr * num
            g = 1.0 - t * t
            hg = thickness * g
            part_s[i, :, c * LANES : (c + 1) * LANES] = e1 * (
                (den * new_den) * (tr + hg) + (num * new_num) * ((tr - hg) * (r * r))
            )
            part_g[i, :, c * LANES : (c + 1) * LANES] = g
            result += [new_num, new_den]
        return tuple(result)

    zero, one = jnp.zeros((SUB, LANES), F32), jnp.ones((SUB, LANES), F32)
    top = lax.fori_loop(0, layers, upward, (zero, one) * len(chunks))
    scale = []
    for c, (f, h) in enumerate(chunks):
        below = 1.0 / (lam[h] * top[2 * c + 1] + top[2 * c])
        scale.append(-lam[h] * below * below)

    def downward(pair, carry):
        i = pair * 2
        result = []
        for c in range(len(chunks)):
            at = slice(c * LANES, (c + 1) * LANES)
            first = part_s[i, :, at] * carry[c]
            now = carry[c] * part_g[i, :, at]
            second = part_s[i + 1, :, at] * now
            sens[pl.ds(pl.multiple_of(pair * 16, 16), 16), at] = jnp.concatenate(
                [first, second], axis=0
            ).astype(BF16)
            result.append(now * part_g[i + 1, :, at])
        return tuple(result)

    lax.fori_loop(0, layers // 2, downward, tuple(scale))

    for other in others:
        copy_a(other, other, other).wait_recv()
    for other in range(offs):
        copy_b(other, other, other).wait_recv()

    lane = lane_index(16)
    tiles = [recv_a[g, 0:16].astype(F32) + recv_b[g].astype(F32) for g in range(offs)]
    pairs = -(-freqs // 2)
    data = [jnp.zeros((16, LANES), F32) for _ in range(pairs)]
    for f in range(freqs):
        placed = jnp.zeros((16, LANES), F32)
        for g in range(offs):
            placed = jnp.where((lane >> 3) == g + f, tiles[g], placed)
        turn = ((f % 2) * 64 - f * SUB) % LANES
        data[f // 2] = data[f // 2] + (pltpu.roll(placed, turn, 1) if turn else placed)
    data = jnp.concatenate(data, axis=1)
    row_weight, row_data = data[0:SUB], data[SUB:16]

    gathered = [recv_a[g, 16:32].astype(F32) for g in range(offs)]
    filt = jnp.concatenate(
        [
            jnp.concatenate([x[h * SUB : (h + 1) * SUB] for x in gathered], axis=0)
            for h in range(halves)
        ],
        axis=1,
    )
    blank = jnp.zeros_like(filt)
    even = jnp.concatenate([filt, blank], axis=0).astype(BF16)
    odd = jnp.concatenate([blank, filt], axis=0).astype(BF16)
    width = halves * LANES

    jac = []
    for p in range(pairs):
        f = 2 * p
        part = nt_dot(sens[:, f * width : (f + 1) * width], even)
        if f + 1 < freqs:
            part = part + nt_dot(sens[:, (f + 1) * width : (f + 2) * width], odd)
        jac.append(part)
    size = layers * SUB
    jac = jnp.concatenate(jac, axis=1)
    cols = pairs * LANES
    weighted = (jac.reshape(layers, SUB, cols) * row_weight[None]).reshape(size, cols)
    upper = weighted.astype(BF16)
    lower = (weighted - upper.astype(F32)).astype(BF16)
    right[0:size] = jac.astype(BF16)
    pad = right.shape[0] - size
    right[size:] = jnp.concatenate([row_data, jnp.zeros((pad - SUB, cols), F32)], axis=0).astype(BF16)
    last = right.shape[0] - LANES
    product = jnp.concatenate(
        [
            nt_dot(upper, right[0:last]),
            nt_dot(upper, right[last:]) + nt_dot(lower, right[last:]),
        ],
        axis=1,
    )
    full = right.shape[0]
    keep = (lax.broadcasted_iota(jnp.int32, (SUB, full), 1) & 7) == lax.broadcasted_iota(
        jnp.int32, (SUB, full), 0
    )
    product = jnp.where(keep[None], product.reshape(layers, SUB, full), 0.0).reshape(size, full)
    product_upper = product.astype(BF16)
    product_lower = (product - product_upper.astype(F32)).astype(BF16)
    out_col = lax.broadcasted_iota(jnp.int32, (LANES, full), 0)
    in_col = lax.broadcasted_iota(jnp.int32, (LANES, full), 1) >> 3
    pick = (in_col == jnp.minimum(out_col, layers)).astype(F32).astype(BF16)
    picked = nt_dot(product_upper, pick) + nt_dot(product_lower, pick)

    lane = lane_index(SUB)
    out = [jnp.zeros((SUB, LANES), F32) for _ in range(-(-layers * layers // LANES))]
    grad = jnp.zeros((SUB, LANES), F32)
    for i in range(layers):
        row = picked[i * SUB : (i + 1) * SUB]
        tile, start = divmod(i * layers, LANES)
        turned = pltpu.roll(row, start, 1) if start else row
        out[tile] = jnp.where((lane >= start) & (lane < start + layers), turned, out[tile])
        if start + layers > LANES:
            out[tile + 1] = jnp.where(lane < start + layers - LANES, turned, out[tile + 1])
        grad = jnp.where(lane == 64 + i, row, grad)
    for tile, value in enumerate(out):
        stop = min(LANES, layers * layers - tile * LANES)
        normal_ref[:, tile * LANES : tile * LANES + stop] = value[:, :stop]
    grad_ref[...] = pltpu.roll(grad, 64, 1)[:, :layers]

    for other in others:
        copy_a(other, off, other).wait_send()
    for other in others + [off]:
        copy_b(other, off, other).wait_send()


def body(earth_model, layer_count, thickness, frequency, midpoint_shift, filters, weights, residual):
    block, layers = earth_model.shape
    taps, offsets = filters.shape
    freqs = frequency.shape[0]
    offs = lax.axis_size("off")
    width = -(-taps // LANES) * LANES
    pairs = -(-freqs // 2)
    full = -(-(layers * SUB + SUB) // LANES) * LANES
    vmem = pl.BlockSpec(memory_space=pltpu.VMEM)
    return pl.pallas_call(
        kernel,
        out_shape=(
            jax.ShapeDtypeStruct((block // offs, layers * layers), F32),
            jax.ShapeDtypeStruct((block // offs, layers), F32),
        ),
        in_specs=[vmem, vmem, vmem, pl.BlockSpec(memory_space=pltpu.SMEM), vmem, vmem, vmem, vmem],
        out_specs=(vmem, vmem),
        scratch_shapes=[
            pltpu.VMEM((LANES, LANES), F32),
            pltpu.VMEM((LANES, 2 * LANES), F32),
            pltpu.VMEM((offs, 32, LANES), BF16),
            pltpu.VMEM((offs, 16, LANES), BF16),
            pltpu.VMEM((offs, 32, LANES), BF16),
            pltpu.VMEM((offs, 16, LANES), BF16),
            pltpu.VMEM((layers, SUB, LANES), F32),
            pltpu.VMEM((layers, SUB, LANES), F32),
            pltpu.VMEM((layers, SUB, freqs * width), F32),
            pltpu.VMEM((layers, SUB, freqs * width), F32),
            pltpu.VMEM((layers * SUB, freqs * width), BF16),
            pltpu.VMEM((full, pairs * LANES), BF16),
            pltpu.SemaphoreType.DMA((offs,)),
            pltpu.SemaphoreType.DMA((offs,)),
            pltpu.SemaphoreType.DMA((offs,)),
            pltpu.SemaphoreType.DMA((offs,)),
        ],
        compiler_params=pltpu.CompilerParams(
            collective_id=0, has_side_effects=True, vmem_limit_bytes=32 * 1024 * 1024
        ),
    )(
        earth_model.T,
        layer_count.reshape(1, -1),
        thickness.reshape(1, -1),
        frequency,
        midpoint_shift.reshape(1, -1),
        filters.T,
        weights,
        residual,
    )


def solution(mesh):
    in_specs = (
        P("shot", None),
        P("shot"),
        P(),
        P(),
        P(),
        P(None, "off"),
        P(None, "off", "shot"),
        P(None, "off", "shot"),
    )
    out_specs = (P(("shot", "off"), None), P(("shot", "off"), None))
    return jax.shard_map(body, mesh=mesh, in_specs=in_specs, out_specs=out_specs, check_vma=False)
```

profile of v0, /device:TPU:30, one launch (start us, length us, event | category | flops | bytes accessed | tf_op | source)
XLA Modules:
  0.0 32.5 jit_solution(3518805617499601524)
XLA Ops:
  0.6 0.0 copy-start.3
  0.6 0.0 copy-start.7
  0.7 0.0 copy-start.4
  0.7 0.0 copy-start.5
  0.7 0.0 copy-start.6
  0.7 0.6 %copy-done.3 = bf16[201,8]{0,1:T(8,128)(2,1)S(1)} copy-done((bf16[201,8]{0,1:T(8,128)(2,1)S(1)}, bf16[201,8]{0,1:T(8,128)(2,1)}, u32[]{:S(2)}) %copy-start.3) | copy-done | bytes 3240
  1.3 0.0 copy-done.7
  1.3 0.0 copy-done.4
  1.3 0.0 copy-done.5
  1.3 0.0 copy-done.6
  1.4 0.0 copy-start
  1.4 0.7 %copy-done = f32[64,40]{0,1:T(8,128)S(1)} copy-done((f32[64,40]{0,1:T(8,128)S(1)}, f32[64,40]{0,1:T(8,128)}, u32[]{:S(2)}) %copy-start) | copy-done | bytes 10264
  2.1 0.0 copy-start.1
  2.1 0.7 %copy-done.1 = bf16[5,8,64]{2,1,0:T(8,128)(2,1)S(1)} copy-done((bf16[5,8,64]{2,1,0:T(8,128)(2,1)S(1)}, bf16[5,8,64]{2,1,0:T(8,128)(2,1)}, u32[]{:S(2)}) %copy-start.1) | copy-done | bytes 5144
  2.8 0.0 copy-start.2
  2.8 0.7 %copy-done.2 = bf16[5,8,64]{2,1,0:T(8,128)(2,1)S(1)} copy-done((bf16[5,8,64]{2,1,0:T(8,128)(2,1)S(1)}, bf16[5,8,64]{2,1,0:T(8,128)(2,1)}, u32[]{:S(2)}) %copy-start.2) | copy-done | bytes 5144
  3.5 27.8 %shard_map.95 = (f32[8,1600]{1,0:T(8,128)S(1)}, f32[8,40]{1,0:T(8,128)S(1)}) custom-call(f32[40,64]{1,0:T(8,128)S(1)} %bitcast.5, s32[1,64]{1,0:T(1,128)S(1)} %bitcast.7, f32[1,40]{1,0:T(1,128)S(1)} %bitcast.8, f32[5]{0:T(128)S(1)} %copy-done.6, s32[1,64]{1,0:T(1,128)S(1)} %bitcast.9, bf16[8,201]{1,0:T(8,128)(2,1)S(1)} %bitcast.6, ...), custom_call_target="tpu_custom_call" | custom-call | tf_op jit(solution)/shard_map/pallas_call | solution.py:296
  31.3 0.6 %copy.12 = f32[8,1600]{1,0:T(8,128)} copy(f32[8,1600]{1,0:T(8,128)S(1)} %get-tuple-element.4) | data formatting | bytes 102400
  32.0 0.6 %copy.13 = f32[8,40]{1,0:T(8,128)} copy(f32[8,40]{1,0:T(8,128)S(1)} %get-tuple-element.5) | data formatting | bytes 2560
Async XLA Ops:
  0.6 0.7 %copy-start.3 = (bf16[201,8]{0,1:T(8,128)(2,1)S(1)}, bf16[201,8]{0,1:T(8,128)(2,1)}, u32[]{:S(2)}) copy-start(bf16[201,8]{0,1:T(8,128)(2,1)} %param.13) | copy-start | bytes 9652
  0.6 0.7 %copy-start.7 = (s32[64]{0:T(128)S(1)}, s32[64]{0:T(128)}, u32[]{:S(2)}) copy-start(s32[64]{0:T(128)} %param.12) | copy-start | bytes 772
  0.7 0.7 %copy-start.4 = (s32[64]{0:T(128)S(1)}, s32[64]{0:T(128)}, u32[]{:S(2)}) copy-start(s32[64]{0:T(128)} %param.9) | copy-start | bytes 772
  0.7 0.7 %copy-start.5 = (f32[40]{0:T(128)S(1)}, f32[40]{0:T(128)}, u32[]{:S(2)}) copy-start(f32[40]{0:T(128)} %param.10) | copy-start | bytes 484
  0.7 0.7 %copy-start.6 = (f32[5]{0:T(128)S(1)}, f32[5]{0:T(128)}, u32[]{:S(2)}) copy-start(f32[5]{0:T(128)} %freq_ref.1) | copy-start | bytes 64
  1.4 0.7 %copy-start = (f32[64,40]{0,1:T(8,128)S(1)}, f32[64,40]{0,1:T(8,128)}, u32[]{:S(2)}) copy-start(f32[64,40]{0,1:T(8,128)} %param.8) | copy-start | bytes 30724
  2.1 0.7 %copy-start.1 = (bf16[5,8,64]{2,1,0:T(8,128)(2,1)S(1)}, bf16[5,8,64]{2,1,0:T(8,128)(2,1)}, u32[]{:S(2)}) copy-start(bf16[5,8,64]{2,1,0:T(8,128)(2,1)} %weight_ref.1) | copy-start | bytes 15364
  2.8 0.7 %copy-start.2 = (bf16[5,8,64]{2,1,0:T(8,128)(2,1)S(1)}, bf16[5,8,64]{2,1,0:T(8,128)(2,1)}, u32[]{:S(2)}) copy-start(bf16[5,8,64]{2,1,0:T(8,128)(2,1)} %resid_ref.1) | copy-start | bytes 15364
where the time goes:
time: 33.1 us; the launch traced here: 32.5 us
  Pallas kernels  27.8 us (84%)
  local copies, waits for them, and re-layouts  4.02 us (12%)
  between operations  0.69 us (2%)
    pallas_call x1, Pallas kernels, body(): pl.pallas_call(kernel, out_shape=(jax.ShapeDtypeStruct((block // offs, la...  27.8 us
    unnamed x18, local copies, waits for them, and re-layouts  4.02 us

commit v1 on v0

--- a/solution.py
+++ b/solution.py
@@ -24,6 +24,16 @@
 
 
 def kernel(
+    model_hbm,
+    count_hbm,
+    thick_hbm,
+    freq_hbm,
+    shift_hbm,
+    filter_hbm,
+    weight_hbm,
+    resid_hbm,
+    normal_ref,
+    grad_ref,
     model_ref,
     count_ref,
     thick_ref,
@@ -32,8 +42,7 @@
     filter_ref,
     weight_ref,
     resid_ref,
-    normal_ref,
-    grad_ref,
+    in_sem,
     small,
     rows,
     send_a,
@@ -61,15 +70,42 @@
     off = lax.axis_index("off")
     before = lax.rem(shot + shots - 1, shots)
     after = lax.rem(shot + 1, shots)
-    others = [lax.rem(off + step, offs) for step in range(1, offs)]
+    reach = [lax.rem((off // 2 + hop) * 2 + (off + core) % 2, offs) for hop in (2, 1, 3, 0) for core in (1, 0)]
+    others = reach[:-1]
+    not_first, not_last = shot > 0, shot < shots - 1
 
     barrier = pltpu.get_barrier_semaphore()
+
+    @pl.when(not_last)
+    def _():
+        for other in reach:
+            pl.semaphore_signal(barrier, inc=1, device_id=(after, other), device_id_type=MESH)
+
     for other in others:
         pl.semaphore_signal(barrier, inc=1, device_id=(shot, other), device_id_type=MESH)
-    for other in range(offs):
-        pl.semaphore_signal(barrier, inc=1, device_id=(after, other), device_id_type=MESH)
+
+    loads = [
+        pltpu.make_async_copy(source, target, in_sem.at[k])
+        for k, (source, target) in enumerate(
+            (
+                (weight_hbm, weight_ref),
+                (resid_hbm, resid_ref),
+                (shift_hbm, shift_ref),
+                (model_hbm, model_ref),
+                (count_hbm, count_ref),
+                (filter_hbm, filter_ref),
+                (thick_hbm, thick_ref),
+                (freq_hbm, freq_ref),
+            )
+        )
+    ]
+    for load in loads:
+        load.start()
 
     small[...] = jnp.zeros_like(small)
+    rows[...] = jnp.zeros_like(rows)
+    for load in loads:
+        load.wait()
     block = model_ref.shape[1]
     small[0:layers, 0:block] = model_ref[...]
     small[layers : layers + 1, 0:block] = count_ref[...].astype(F32)
@@ -79,7 +115,6 @@
     shift = own[:, layers + 1 : layers + 2].astype(jnp.int32)
     shift = jnp.broadcast_to(shift, (SUB, LANES))
 
-    rows[...] = jnp.zeros_like(rows)
     bits = [(shift & (1 << b)) != 0 for b in range(7)]
     for q, ref in enumerate((weight_ref, resid_ref)):
         for f in range(freqs):
@@ -94,16 +129,20 @@
     columns = jnp.concatenate([columns, jnp.zeros((SUB, halves * LANES - taps), F32)], axis=1)
     columns = jnp.concatenate([columns[:, h * LANES : (h + 1) * LANES] for h in range(halves)], axis=0)
     columns = columns.astype(BF16)
-    has_before = shot > 0
     for j in range(offs):
         at = slice(j * SUB, (j + 1) * SUB)
         send_a[j, 0:16] = jnp.concatenate([by_weight[at], by_resid[at]], axis=0).astype(BF16)
         send_a[j, 16:32] = columns
         at = slice(offs * SUB + j * SUB, offs * SUB + (j + 1) * SUB)
-        tile = jnp.concatenate([by_weight[at], by_resid[at]], axis=0)
-        send_b[j] = jnp.where(has_before, tile, 0.0).astype(BF16)
-
-    pl.semaphore_wait(barrier, 2 * offs - 1)
+        send_b[j] = jnp.concatenate([by_weight[at], by_resid[at]], axis=0).astype(BF16)
+
+    @pl.when(not_first)
+    def _():
+        pl.semaphore_wait(barrier, 2 * offs - 1)
+
+    @pl.when(jnp.logical_not(not_first))
+    def _():
+        pl.semaphore_wait(barrier, offs - 1)
 
     def copy_a(source, slot, device):
         return pltpu.make_async_remote_copy(
@@ -125,10 +164,21 @@
             device_id_type=MESH,
         )
 
-    for other in others:
+    @pl.when(not_first)
+    def _():
+        for other in reach[:2]:
+            copy_b(other, off, other).start()
+
+    for other in others[:2]:
         copy_a(other, off, other).start()
-    for other in others + [off]:
-        copy_b(other, off, other).start()
+
+    @pl.when(not_first)
+    def _():
+        for other in reach[2:]:
+            copy_b(other, off, other).start()
+
+    for other in others[2:]:
+        copy_a(other, off, other).start()
     recv_a[off] = send_a[off]
 
     layer = lane_index(SUB)
@@ -145,7 +195,7 @@
         tap = jnp.minimum(layer + h * LANES, taps - 1).astype(F32)
         lam.append(jnp.exp(-3.0 + 6.0 * tap / (taps - 1)))
     lam2 = [x * x for x in lam]
-    omega = [freq_ref[f] for f in range(freqs)]
+    omega = [jnp.broadcast_to(freq_ref[0:1, f : f + 1], (SUB, LANES)) for f in range(freqs)]
     chunks = [(f, h) for f in range(freqs) for h in range(halves)]
 
     def upward(step, carry):
@@ -197,8 +247,15 @@
 
     for other in others:
         copy_a(other, other, other).wait_recv()
-    for other in range(offs):
-        copy_b(other, other, other).wait_recv()
+
+    @pl.when(not_last)
+    def _():
+        for other in reach:
+            copy_b(other, other, other).wait_recv()
+
+    @pl.when(jnp.logical_not(not_last))
+    def _():
+        recv_b[...] = jnp.zeros_like(recv_b)
 
     lane = lane_index(16)
     tiles = [recv_a[g, 0:16].astype(F32) + recv_b[g].astype(F32) for g in range(offs)]
@@ -280,8 +337,22 @@
 
     for other in others:
         copy_a(other, off, other).wait_send()
-    for other in others + [off]:
-        copy_b(other, off, other).wait_send()
+
+    @pl.when(not_first)
+    def _():
+        for other in reach:
+            copy_b(other, off, other).wait_send()
+
+
+def hand_over(normal_in, grad_in, normal_out, grad_out, sem):
+    copies = [
+        pltpu.make_async_copy(normal_in, normal_out, sem.at[0]),
+        pltpu.make_async_copy(grad_in, grad_out, sem.at[1]),
+    ]
+    for copy in copies:
+        copy.start()
+    for copy in copies:
+        copy.wait()
 
 
 def body(earth_model, layer_count, thickness, frequency, midpoint_shift, filters, weights, residual):
@@ -293,15 +364,28 @@
     pairs = -(-freqs // 2)
     full = -(-(layers * SUB + SUB) // LANES) * LANES
     vmem = pl.BlockSpec(memory_space=pltpu.VMEM)
-    return pl.pallas_call(
+    operands = (
+        earth_model.T,
+        layer_count.reshape(1, -1),
+        thickness.reshape(1, -1),
+        frequency.reshape(1, -1),
+        midpoint_shift.reshape(1, -1),
+        filters.T,
+        weights,
+        residual,
+    )
+    operands = tuple(pltpu.with_memory_space_constraint(x, pltpu.HBM) for x in operands)
+    results = pl.pallas_call(
         kernel,
         out_shape=(
-            jax.ShapeDtypeStruct((block // offs, layers * layers), F32),
-            jax.ShapeDtypeStruct((block // offs, layers), F32),
+            pltpu.VMEM((block // offs, layers * layers), F32),
+            pltpu.VMEM((block // offs, layers), F32),
         ),
-        in_specs=[vmem, vmem, vmem, pl.BlockSpec(memory_space=pltpu.SMEM), vmem, vmem, vmem, vmem],
+        in_specs=[pl.BlockSpec(memory_space=pltpu.HBM)] * len(operands),
         out_specs=(vmem, vmem),
-        scratch_shapes=[
+        scratch_shapes=[pltpu.VMEM(x.shape, x.dtype) for x in operands]
+        + [
+            pltpu.SemaphoreType.DMA((len(operands),)),
             pltpu.VMEM((LANES, LANES), F32),
             pltpu.VMEM((LANES, 2 * LANES), F32),
             pltpu.VMEM((offs, 32, LANES), BF16),
@@ -322,16 +406,15 @@
         compiler_params=pltpu.CompilerParams(
             collective_id=0, has_side_effects=True, vmem_limit_bytes=32 * 1024 * 1024
         ),
-    )(
-        earth_model.T,
-        layer_count.reshape(1, -1),
-        thickness.reshape(1, -1),
-        frequency,
-        midpoint_shift.reshape(1, -1),
-        filters.T,
-        weights,
-        residual,
-    )
+    )(*operands)
+    results = tuple(pltpu.with_memory_space_constraint(x, pltpu.VMEM) for x in results)
+    return pl.pallas_call(
+        hand_over,
+        out_shape=tuple(pltpu.HBM(x.shape, x.dtype) for x in results),
+        in_specs=[vmem] * len(results),
+        out_specs=(pl.BlockSpec(memory_space=pltpu.HBM),) * len(results),
+        scratch_shapes=[pltpu.SemaphoreType.DMA((len(results),))],
+    )(*results)
 
 
 def solution(mesh):

time: 33.1 us -> 27.4 us (0.83); the launches traced: 32.5 us -> 27.2 us
  local copies, waits for them, and re-layouts: 4.02 us -> 0 us
  Pallas kernels: 27.8 us -> 26.6 us
    unnamed x18 -> x0, local copies, waits for them, and re-layouts: 4.02 us -> none
    pallas_call x1 -> x2, Pallas kernels: 27.8 us -> 26.6 us  [the longest x1 26 us: body(): pl.pallas_call(kernel, out_shape=(pltpu.VMEM((block // offs, layers * lay...]
where the time goes in v1:
time: 27.4 us; the launch traced here: 27.2 us
  Pallas kernels  26.6 us (97%)
  between operations  0.64 us (2%)
    pallas_call x1, Pallas kernels, body(): pl.pallas_call(kernel, out_shape=(pltpu.VMEM((block // offs, layers * lay...  26 us
    pallas_call x1, Pallas kernels, body(): pl.pallas_call(hand_over, out_shape=tuple((pltpu.HBM(x.shape, x.dtype) fo...  0.64 us

profile of v1, /device:TPU:30, one launch (start us, length us, event | category | flops | bytes accessed | tf_op | source)
XLA Modules:
  0.0 27.2 jit_solution(7406920658186356338)
XLA Ops:
  0.6 26.0 %shard_map.95 = (f32[8,1600]{1,0:T(8,128)S(1)}, f32[8,40]{1,0:T(8,128)S(1)}) custom-call(f32[40,64]{1,0:T(8,128)} %bitcast.6, s32[1,64]{1,0:T(1,128)} %bitcast.8, f32[1,40]{1,0:T(1,128)} %bitcast.9, f32[1,5]{1,0:T(1,128)} %bitcast.10, s32[1,64]{1,0:T(1,128)} %bitcast.11, bf16[8,201]{1,0:T(8,128)(2,1)} %bitcast.7, bf16[5,8,64]{2,1,0:T(8,128)(2,1)} %weight_hbm.1, ...), custom_call_target="tpu_custom_call" | custom-call | tf_op jit(solution)/shard_map/pallas_call | solution.py:378
  26.6 0.6 %shard_map.96 = (f32[8,1600]{1,0:T(8,128)}, f32[8,40]{1,0:T(8,128)}) custom-call(f32[8,1600]{1,0:T(8,128)S(1)} %get-tuple-element.4.normal_in, f32[8,40]{1,0:T(8,128)S(1)} %get-tuple-element.5.grad_in), custom_call_target="tpu_custom_call" | custom-call | tf_op jit(solution)/shard_map/pallas_call | solution.py:411

commit v2 on v1

--- a/solution.py
+++ b/solution.py
@@ -21,6 +21,11 @@
 
 def lane_index(rows, lanes=LANES):
     return lax.broadcasted_iota(jnp.int32, (rows, lanes), 1)
+
+
+def leads(quarter, other):
+    rank = lambda q: q + (q == 2).astype(jnp.int32) - (q == 3).astype(jnp.int32)
+    return rank(quarter) > rank(other)
 
 
 def kernel(
@@ -70,19 +75,36 @@
     off = lax.axis_index("off")
     before = lax.rem(shot + shots - 1, shots)
     after = lax.rem(shot + 1, shots)
-    reach = [lax.rem((off // 2 + hop) * 2 + (off + core) % 2, offs) for hop in (2, 1, 3, 0) for core in (1, 0)]
-    others = reach[:-1]
+    block_z, core = off // 2, lax.rem(off, 2)
+    sides = (lax.rem(core + 1, 2), core)
+    hops = [lax.rem(block_z + hop, 4) for hop in (2, 1, 3)]
+    pair = lambda quarter: [quarter * 2 + side for side in sides]
     not_first, not_last = shot > 0, shot < shots - 1
+    sibling = block_z * 2 + sides[0]
 
     barrier = pltpu.get_barrier_semaphore()
+
+    def announce(at_shot, device):
+        pl.semaphore_signal(barrier, inc=1, device_id=(at_shot, device), device_id_type=MESH)
+
+    for quarter in hops:
+
+        @pl.when(leads(quarter, block_z))
+        def _():
+            for device in pair(quarter):
+                announce(shot, device)
+
+            @pl.when(not_last)
+            def _():
+                for device in pair(quarter):
+                    announce(after, device)
+
+    announce(shot, sibling)
 
     @pl.when(not_last)
     def _():
-        for other in reach:
-            pl.semaphore_signal(barrier, inc=1, device_id=(after, other), device_id_type=MESH)
-
-    for other in others:
-        pl.semaphore_signal(barrier, inc=1, device_id=(shot, other), device_id_type=MESH)
+        for device in pair(block_z):
+            announce(after, device)
 
     loads = [
         pltpu.make_async_copy(source, target, in_sem.at[k])
@@ -91,9 +113,9 @@
                 (weight_hbm, weight_ref),
                 (resid_hbm, resid_ref),
                 (shift_hbm, shift_ref),
+                (filter_hbm, filter_ref),
                 (model_hbm, model_ref),
                 (count_hbm, count_ref),
-                (filter_hbm, filter_ref),
                 (thick_hbm, thick_ref),
                 (freq_hbm, freq_ref),
             )
@@ -102,18 +124,14 @@
     for load in loads:
         load.start()
 
-    small[...] = jnp.zeros_like(small)
     rows[...] = jnp.zeros_like(rows)
-    for load in loads:
+    for load in loads[:3]:
         load.wait()
-    block = model_ref.shape[1]
-    small[0:layers, 0:block] = model_ref[...]
-    small[layers : layers + 1, 0:block] = count_ref[...].astype(F32)
-    small[layers + 1 : layers + 2, 0 : shift_ref.shape[1]] = shift_ref[...].astype(F32)
-    small[...] = small[...].T
-    own = small[pl.ds(pl.multiple_of(off * SUB, SUB), SUB), :]
-    shift = own[:, layers + 1 : layers + 2].astype(jnp.int32)
-    shift = jnp.broadcast_to(shift, (SUB, LANES))
+    layer = lane_index(SUB)
+    own_offset = layer == off * SUB + lax.broadcasted_iota(jnp.int32, (SUB, LANES), 0)
+    shift = jnp.concatenate([shift_ref[...], jnp.zeros((1, LANES - shift_ref.shape[1]), jnp.int32)], axis=1)
+    shift = jnp.where(own_offset, jnp.broadcast_to(shift, (SUB, LANES)).astype(F32), 0.0)
+    shift = jnp.broadcast_to(jnp.sum(shift, axis=1, keepdims=True), (SUB, LANES)).astype(jnp.int32)
 
     bits = [(shift & (1 << b)) != 0 for b in range(7)]
     for q, ref in enumerate((weight_ref, resid_ref)):
@@ -122,27 +140,19 @@
             x = jnp.concatenate([x, jnp.zeros((SUB, LANES - x.shape[1]), F32)], axis=1)
             for b in range(7):
                 x = jnp.where(bits[b], pltpu.roll(x, LANES - (1 << b), 1), x)
-            rows[pl.ds(pl.multiple_of((off + f) * SUB, SUB), SUB), q * LANES : (q + 1) * LANES] = x
-    by_weight = rows[:, 0:LANES].T
-    by_resid = rows[:, LANES : 2 * LANES].T
+            rows[pl.ds(pl.multiple_of(lax.rem(off + f + q * 8, 16) * SUB, SUB), SUB), :] = x
+    moved = rows[...].T
+    loads[3].wait()
     columns = filter_ref[...].astype(F32)
-    columns = jnp.concatenate([columns, jnp.zeros((SUB, halves * LANES - taps), F32)], axis=1)
-    columns = jnp.concatenate([columns[:, h * LANES : (h + 1) * LANES] for h in range(halves)], axis=0)
-    columns = columns.astype(BF16)
+    columns = jnp.concatenate([columns, jnp.zeros((SUB, halves * LANES - taps), F32)], axis=1).astype(BF16)
     for j in range(offs):
-        at = slice(j * SUB, (j + 1) * SUB)
-        send_a[j, 0:16] = jnp.concatenate([by_weight[at], by_resid[at]], axis=0).astype(BF16)
-        send_a[j, 16:32] = columns
-        at = slice(offs * SUB + j * SUB, offs * SUB + (j + 1) * SUB)
-        send_b[j] = jnp.concatenate([by_weight[at], by_resid[at]], axis=0).astype(BF16)
-
-    @pl.when(not_first)
-    def _():
-        pl.semaphore_wait(barrier, 2 * offs - 1)
-
-    @pl.when(jnp.logical_not(not_first))
-    def _():
-        pl.semaphore_wait(barrier, offs - 1)
+        send_a[j, 0] = moved[j * SUB : (j + 1) * SUB].astype(BF16)
+        for h in range(halves):
+            send_a[j, 1 + h] = columns[:, h * LANES : (h + 1) * LANES]
+        send_b[j] = moved[(offs + j) * SUB : (offs + j + 1) * SUB].astype(BF16)
+
+    led = sum(leads(block_z, quarter).astype(jnp.int32) for quarter in hops)
+    pl.semaphore_wait(barrier, 2 * led + 1 + not_first.astype(jnp.int32) * (2 * led + 2))
 
     def copy_a(source, slot, device):
         return pltpu.make_async_remote_copy(
@@ -164,24 +174,38 @@
             device_id_type=MESH,
         )
 
+    def send_to(quarter):
+        @pl.when(not_first)
+        def _():
+            for device in pair(quarter):
+                copy_b(device, off, device).start()
+
+        for device in pair(quarter):
+            copy_a(device, off, device).start()
+
+    for quarter in hops:
+
+        @pl.when(leads(block_z, quarter))
+        def _():
+            send_to(quarter)
+
     @pl.when(not_first)
     def _():
-        for other in reach[:2]:
-            copy_b(other, off, other).start()
-
-    for other in others[:2]:
-        copy_a(other, off, other).start()
-
-    @pl.when(not_first)
-    def _():
-        for other in reach[2:]:
-            copy_b(other, off, other).start()
-
-    for other in others[2:]:
-        copy_a(other, off, other).start()
+        for device in pair(block_z):
+            copy_b(device, off, device).start()
+
+    copy_a(sibling, off, sibling).start()
     recv_a[off] = send_a[off]
 
-    layer = lane_index(SUB)
+    for load in loads[4:]:
+        load.wait()
+    small[...] = jnp.zeros_like(small)
+    block = model_ref.shape[1]
+    small[0:layers, 0:block] = model_ref[...]
+    small[layers : layers + 1, 0:block] = count_ref[...].astype(F32)
+    small[...] = small[...].T
+    own = small[pl.ds(pl.multiple_of(off * SUB, SUB), SUB), :]
+
     count = jnp.broadcast_to(own[:, layers : layers + 1], (SUB, LANES)).astype(jnp.int32)
     thick = jnp.concatenate([thick_ref[...], jnp.zeros((1, LANES - layers), F32)], axis=1)
     thick = jnp.broadcast_to(thick, (SUB, LANES))
@@ -245,35 +269,43 @@
 
     lax.fori_loop(0, layers // 2, downward, tuple(scale))
 
-    for other in others:
-        copy_a(other, other, other).wait_recv()
+    for quarter in (hops[1], hops[2], hops[0]):
+        for device in pair(quarter):
+            copy_a(device, device, device).wait_recv()
+
+        @pl.when(jnp.logical_not(leads(block_z, quarter)))
+        def _():
+            send_to(quarter)
+
+    copy_a(sibling, sibling, sibling).wait_recv()
 
     @pl.when(not_last)
     def _():
-        for other in reach:
-            copy_b(other, other, other).wait_recv()
+        for quarter in [block_z] + hops:
+            for device in pair(quarter):
+                copy_b(device, device, device).wait_recv()
 
     @pl.when(jnp.logical_not(not_last))
     def _():
         recv_b[...] = jnp.zeros_like(recv_b)
 
-    lane = lane_index(16)
-    tiles = [recv_a[g, 0:16].astype(F32) + recv_b[g].astype(F32) for g in range(offs)]
+    lane = lane_index(SUB)
+    tiles = [recv_a[g, 0].astype(F32) + recv_b[g].astype(F32) for g in range(offs)]
     pairs = -(-freqs // 2)
-    data = [jnp.zeros((16, LANES), F32) for _ in range(pairs)]
-    for f in range(freqs):
-        placed = jnp.zeros((16, LANES), F32)
-        for g in range(offs):
-            placed = jnp.where((lane >> 3) == g + f, tiles[g], placed)
-        turn = ((f % 2) * 64 - f * SUB) % LANES
-        data[f // 2] = data[f // 2] + (pltpu.roll(placed, turn, 1) if turn else placed)
-    data = jnp.concatenate(data, axis=1)
-    row_weight, row_data = data[0:SUB], data[SUB:16]
-
-    gathered = [recv_a[g, 16:32].astype(F32) for g in range(offs)]
+    data = [[jnp.zeros((SUB, LANES), F32) for _ in range(pairs)] for _ in range(2)]
+    for q in range(2):
+        for f in range(freqs):
+            placed = jnp.zeros((SUB, LANES), F32)
+            for g in range(offs):
+                placed = jnp.where((lane >> 3) == (g + f + q * 8) % 16, tiles[g], placed)
+            turn = ((f % 2 + q) * 64 - f * SUB) % LANES
+            data[q][f // 2] = data[q][f // 2] + (pltpu.roll(placed, turn, 1) if turn else placed)
+    row_weight, row_data = (jnp.concatenate(x, axis=1) for x in data)
+
+    gathered = [[recv_a[g, 1 + h].astype(F32) for h in range(halves)] for g in range(offs)]
     filt = jnp.concatenate(
         [
-            jnp.concatenate([x[h * SUB : (h + 1) * SUB] for x in gathered], axis=0)
+            jnp.concatenate([x[h] for x in gathered], axis=0)
             for h in range(halves)
         ],
         axis=1,
@@ -335,13 +367,16 @@
         normal_ref[:, tile * LANES : tile * LANES + stop] = value[:, :stop]
     grad_ref[...] = pltpu.roll(grad, 64, 1)[:, :layers]
 
-    for other in others:
-        copy_a(other, off, other).wait_send()
+    for quarter in hops:
+        for device in pair(quarter):
+            copy_a(device, off, device).wait_send()
+    copy_a(sibling, off, sibling).wait_send()
 
     @pl.when(not_first)
     def _():
-        for other in reach:
-            copy_b(other, off, other).wait_send()
+        for quarter in [block_z] + hops:
+            for device in pair(quarter):
+                copy_b(device, off, device).wait_send()
 
 
 def hand_over(normal_in, grad_in, normal_out, grad_out, sem):
@@ -387,11 +422,11 @@
         + [
             pltpu.SemaphoreType.DMA((len(operands),)),
             pltpu.VMEM((LANES, LANES), F32),
-            pltpu.VMEM((LANES, 2 * LANES), F32),
-            pltpu.VMEM((offs, 32, LANES), BF16),
-            pltpu.VMEM((offs, 16, LANES), BF16),
-            pltpu.VMEM((offs, 32, LANES), BF16),
-            pltpu.VMEM((offs, 16, LANES), BF16),
+            pltpu.VMEM((LANES, LANES), F32),
+            pltpu.VMEM((offs, 1 + width // LANES, SUB, LANES), BF16),
+            pltpu.VMEM((offs, SUB, LANES), BF16),
+            pltpu.VMEM((offs, 1 + width // LANES, SUB, LANES), BF16),
+            pltpu.VMEM((offs, SUB, LANES), BF16),
             pltpu.VMEM((layers, SUB, LANES), F32),
             pltpu.VMEM((layers, SUB, LANES), F32),
             pltpu.VMEM((layers, SUB, freqs * width), F32),

time: 27.4 us -> 25.4 us (0.927)
  the two profiles are of different devices: /device:TPU:30 before, /device:TPU:480 now
where the time goes in v2:
time: 25.4 us; the launch traced here: 25.3 us
  Pallas kernels  24.6 us (97%)
  between operations  0.64 us (3%)
    pallas_call x1, Pallas kernels, body(): pl.pallas_call(kernel, out_shape=(pltpu.VMEM((block // offs, layers * lay...  24 us
    pallas_call x1, Pallas kernels, body(): pl.pallas_call(hand_over, out_shape=tuple((pltpu.HBM(x.shape, x.dtype) fo...  0.64 us

profile of v2, /device:TPU:480, one launch (start us, length us, event | category | flops | bytes accessed | tf_op | source)
XLA Modules:
  0.0 25.3 jit_solution(3219479849007247981)
XLA Ops:
  0.6 24.0 %shard_map.95 = (f32[8,1600]{1,0:T(8,128)S(1)}, f32[8,40]{1,0:T(8,128)S(1)}) custom-call(f32[40,64]{1,0:T(8,128)} %bitcast.6, s32[1,64]{1,0:T(1,128)} %bitcast.8, f32[1,40]{1,0:T(1,128)} %bitcast.9, f32[1,5]{1,0:T(1,128)} %bitcast.10, s32[1,64]{1,0:T(1,128)} %bitcast.11, bf16[8,201]{1,0:T(8,128)(2,1)} %bitcast.7, bf16[5,8,64]{2,1,0:T(8,128)(2,1)} %weight_hbm.1, ...), custom_call_target="tpu_custom_call" | custom-call | tf_op jit(solution)/shard_map/pallas_call | solution.py:413
  24.6 0.6 %shard_map.96 = (f32[8,1600]{1,0:T(8,128)}, f32[8,40]{1,0:T(8,128)}) custom-call(f32[8,1600]{1,0:T(8,128)S(1)} %get-tuple-element.4.normal_in, f32[8,40]{1,0:T(8,128)S(1)} %get-tuple-element.5.grad_in), custom_call_target="tpu_custom_call" | custom-call | tf_op jit(solution)/shard_map/pallas_call | solution.py:446

commit v3 on v2

--- a/solution.py
+++ b/solution.py
@@ -23,9 +23,15 @@
     return lax.broadcasted_iota(jnp.int32, (rows, lanes), 1)
 
 
+LEADS = 0x3bde
+
+
 def leads(quarter, other):
-    rank = lambda q: q + (q == 2).astype(jnp.int32) - (q == 3).astype(jnp.int32)
-    return rank(quarter) > rank(other)
+    return ((LEADS >> (quarter * 4 + other)) & 1) != 0
+
+
+def is_early(quarter):
+    return quarter < 2
 
 
 def kernel(
@@ -64,6 +70,7 @@
     send_sem_b,
     recv_sem_a,
     recv_sem_b,
+    go_sem,
 ):
     layers = model_ref.shape[0]
     freqs = weight_ref.shape[0]
@@ -94,10 +101,10 @@
             for device in pair(quarter):
                 announce(shot, device)
 
-            @pl.when(not_last)
-            def _():
-                for device in pair(quarter):
-                    announce(after, device)
+        @pl.when(leads(quarter, block_z) & is_early(block_z) & not_last)
+        def _():
+            for device in pair(quarter):
+                announce(after, device)
 
     announce(shot, sibling)
 
@@ -105,6 +112,10 @@
     def _():
         for device in pair(block_z):
             announce(after, device)
+
+    @pl.when(not_first)
+    def _():
+        announce(before, off)
 
     loads = [
         pltpu.make_async_copy(source, target, in_sem.at[k])
@@ -152,7 +163,18 @@
         send_b[j] = moved[(offs + j) * SUB : (offs + j + 1) * SUB].astype(BF16)
 
     led = sum(leads(block_z, quarter).astype(jnp.int32) for quarter in hops)
-    pl.semaphore_wait(barrier, 2 * led + 1 + not_first.astype(jnp.int32) * (2 * led + 2))
+    led_early = sum((leads(block_z, quarter) & is_early(quarter)).astype(jnp.int32) for quarter in hops)
+    pl.semaphore_wait(
+        barrier,
+        2 * led
+        + 1
+        + not_first.astype(jnp.int32) * (2 * led_early + 2)
+        + not_last.astype(jnp.int32),
+    )
+
+    @pl.when(not_last)
+    def _():
+        pl.semaphore_signal(go_sem, inc=1, device_id=(after, off), device_id_type=MESH)
 
     def copy_a(source, slot, device):
         return pltpu.make_async_remote_copy(
@@ -174,20 +196,23 @@
             device_id_type=MESH,
         )
 
-    def send_to(quarter):
-        @pl.when(not_first)
-        def _():
-            for device in pair(quarter):
-                copy_b(device, off, device).start()
-
+    def send_a_to(quarter):
         for device in pair(quarter):
             copy_a(device, off, device).start()
 
+    def send_b_to(quarter):
+        for device in pair(quarter):
+            copy_b(device, off, device).start()
+
     for quarter in hops:
 
+        @pl.when(leads(block_z, quarter) & is_early(quarter) & not_first)
+        def _():
+            send_b_to(quarter)
+
         @pl.when(leads(block_z, quarter))
         def _():
-            send_to(quarter)
+            send_a_to(quarter)
 
     @pl.when(not_first)
     def _():
@@ -269,13 +294,37 @@
 
     lax.fori_loop(0, layers // 2, downward, tuple(scale))
 
-    for quarter in (hops[1], hops[2], hops[0]):
+    @pl.when(not_first)
+    def _():
+        pl.semaphore_wait(go_sem, 1)
+
+    for quarter in hops:
+
+        @pl.when(leads(block_z, quarter) & jnp.logical_not(is_early(quarter)) & not_first)
+        def _():
+            send_b_to(quarter)
+
+    def arrived(quarter):
         for device in pair(quarter):
             copy_a(device, device, device).wait_recv()
 
+    in_turn = (hops[1], hops[2], hops[0])
+    for quarter in in_turn:
+
         @pl.when(jnp.logical_not(leads(block_z, quarter)))
         def _():
-            send_to(quarter)
+            arrived(quarter)
+            send_a_to(quarter)
+
+            @pl.when(not_first)
+            def _():
+                send_b_to(quarter)
+
+    for quarter in in_turn:
+
+        @pl.when(leads(block_z, quarter))
+        def _():
+            arrived(quarter)
 
     copy_a(sibling, sibling, sibling).wait_recv()
 
@@ -437,6 +486,7 @@
             pltpu.SemaphoreType.DMA((offs,)),
             pltpu.SemaphoreType.DMA((offs,)),
             pltpu.SemaphoreType.DMA((offs,)),
+            pltpu.SemaphoreType.REGULAR,
         ],
         compiler_params=pltpu.CompilerParams(
             collective_id=0, has_side_effects=True, vmem_limit_bytes=32 * 1024 * 1024

time: 25.4 us -> 24 us (0.945)
  the two profiles are of different devices: /device:TPU:480 before, /device:TPU:30 now
where the time goes in v3:
time: 24 us; the launch traced here: 23.8 us
  Pallas kernels  23.1 us (96%)
  between operations  0.64 us (3%)
    pallas_call x1, Pallas kernels, body(): pl.pallas_call(kernel, out_shape=(pltpu.VMEM((block // offs, layers * lay...  22.5 us
    pallas_call x1, Pallas kernels, body(): pl.pallas_call(hand_over, out_shape=tuple((pltpu.HBM(x.shape, x.dtype) fo...  0.64 us

profile of v3, /device:TPU:30, one launch (start us, length us, event | category | flops | bytes accessed | tf_op | source)
XLA Modules:
  0.0 23.8 jit_solution(9122900078177212021)
XLA Ops:
  0.6 22.5 %shard_map.95 = (f32[8,1600]{1,0:T(8,128)S(1)}, f32[8,40]{1,0:T(8,128)S(1)}) custom-call(f32[40,64]{1,0:T(8,128)} %bitcast.6, s32[1,64]{1,0:T(1,128)} %bitcast.8, f32[1,40]{1,0:T(1,128)} %bitcast.9, f32[1,5]{1,0:T(1,128)} %bitcast.10, s32[1,64]{1,0:T(1,128)} %bitcast.11, bf16[8,201]{1,0:T(8,128)(2,1)} %bitcast.7, bf16[5,8,64]{2,1,0:T(8,128)(2,1)} %weight_hbm.1, ...), custom_call_target="tpu_custom_call" | custom-call | tf_op jit(solution)/shard_map/pallas_call | solution.py:462
  23.1 0.6 %shard_map.96 = (f32[8,1600]{1,0:T(8,128)}, f32[8,40]{1,0:T(8,128)}) custom-call(f32[8,1600]{1,0:T(8,128)S(1)} %get-tuple-element.4.normal_in, f32[8,40]{1,0:T(8,128)S(1)} %get-tuple-element.5.grad_in), custom_call_target="tpu_custom_call" | custom-call | tf_op jit(solution)/shard_map/pallas_call | solution.py:496

commit v4 on v3

--- a/solution.py
+++ b/solution.py
@@ -21,13 +21,6 @@
 
 def lane_index(rows, lanes=LANES):
     return lax.broadcasted_iota(jnp.int32, (rows, lanes), 1)
-
-
-LEADS = 0x3bde
-
-
-def leads(quarter, other):
-    return ((LEADS >> (quarter * 4 + other)) & 1) != 0
 
 
 def is_early(quarter):
@@ -95,23 +88,15 @@
         pl.semaphore_signal(barrier, inc=1, device_id=(at_shot, device), device_id_type=MESH)
 
     for quarter in hops:
-
-        @pl.when(leads(quarter, block_z))
-        def _():
-            for device in pair(quarter):
-                announce(shot, device)
-
-        @pl.when(leads(quarter, block_z) & is_early(block_z) & not_last)
-        def _():
+        for device in pair(quarter):
+            announce(shot, device)
+    announce(shot, sibling)
+
+    @pl.when(not_last & is_early(block_z))
+    def _():
+        for quarter in hops + [block_z]:
             for device in pair(quarter):
                 announce(after, device)
-
-    announce(shot, sibling)
-
-    @pl.when(not_last)
-    def _():
-        for device in pair(block_z):
-            announce(after, device)
 
     @pl.when(not_first)
     def _():
@@ -162,14 +147,8 @@
             send_a[j, 1 + h] = columns[:, h * LANES : (h + 1) * LANES]
         send_b[j] = moved[(offs + j) * SUB : (offs + j + 1) * SUB].astype(BF16)
 
-    led = sum(leads(block_z, quarter).astype(jnp.int32) for quarter in hops)
-    led_early = sum((leads(block_z, quarter) & is_early(quarter)).astype(jnp.int32) for quarter in hops)
     pl.semaphore_wait(
-        barrier,
-        2 * led
-        + 1
-        + not_first.astype(jnp.int32) * (2 * led_early + 2)
-        + not_last.astype(jnp.int32),
+        barrier, offs - 1 + not_first.astype(jnp.int32) * (offs // 2) + not_last.astype(jnp.int32)
     )
 
     @pl.when(not_last)
@@ -206,18 +185,15 @@
 
     for quarter in hops:
 
-        @pl.when(leads(block_z, quarter) & is_early(quarter) & not_first)
+        @pl.when(is_early(quarter) & not_first)
         def _():
             send_b_to(quarter)
 
-        @pl.when(leads(block_z, quarter))
-        def _():
-            send_a_to(quarter)
-
-    @pl.when(not_first)
-    def _():
-        for device in pair(block_z):
-            copy_b(device, off, device).start()
+        send_a_to(quarter)
+
+    @pl.when(is_early(block_z) & not_first)
+    def _():
+        send_b_to(block_z)
 
     copy_a(sibling, off, sibling).start()
     recv_a[off] = send_a[off]
@@ -298,34 +274,15 @@
     def _():
         pl.semaphore_wait(go_sem, 1)
 
-    for quarter in hops:
-
-        @pl.when(leads(block_z, quarter) & jnp.logical_not(is_early(quarter)) & not_first)
+    for quarter in [block_z] + hops:
+
+        @pl.when(jnp.logical_not(is_early(quarter)) & not_first)
         def _():
             send_b_to(quarter)
 
-    def arrived(quarter):
+    for quarter in hops:
         for device in pair(quarter):
             copy_a(device, device, device).wait_recv()
-
-    in_turn = (hops[1], hops[2], hops[0])
-    for quarter in in_turn:
-
-        @pl.when(jnp.logical_not(leads(block_z, quarter)))
-        def _():
-            arrived(quarter)
-            send_a_to(quarter)
-
-            @pl.when(not_first)
-            def _():
-                send_b_to(quarter)
-
-    for quarter in in_turn:
-
-        @pl.when(leads(block_z, quarter))
-        def _():
-            arrived(quarter)
-
     copy_a(sibling, sibling, sibling).wait_recv()
 
     @pl.when(not_last)

time: 24 us -> 23.4 us (0.975)
  Pallas kernels: 23.1 us -> 22.4 us
    pallas_call x1, Pallas kernels: 22.5 us -> 21.7 us  [body(): pl.pallas_call(kernel, out_shape=(pltpu.VMEM((block // offs, layers * lay...]
where the time goes in v4:
time: 23.4 us; the launch traced here: 23 us
  Pallas kernels  22.4 us (96%)
  between operations  0.64 us (3%)
    pallas_call x1, Pallas kernels, body(): pl.pallas_call(kernel, out_shape=(pltpu.VMEM((block // offs, layers * lay...  21.7 us
    pallas_call x1, Pallas kernels, body(): pl.pallas_call(hand_over, out_shape=tuple((pltpu.HBM(x.shape, x.dtype) fo...  0.64 us

profile of v4, /device:TPU:30, one launch (start us, length us, event | category | flops | bytes accessed | tf_op | source)
XLA Modules:
  0.0 23.0 jit_solution(6410787181253151492)
XLA Ops:
  0.6 21.7 %shard_map.95 = (f32[8,1600]{1,0:T(8,128)S(1)}, f32[8,40]{1,0:T(8,128)S(1)}) custom-call(f32[40,64]{1,0:T(8,128)} %bitcast.6, s32[1,64]{1,0:T(1,128)} %bitcast.8, f32[1,40]{1,0:T(1,128)} %bitcast.9, f32[1,5]{1,0:T(1,128)} %bitcast.10, s32[1,64]{1,0:T(1,128)} %bitcast.11, bf16[8,201]{1,0:T(8,128)(2,1)} %bitcast.7, bf16[5,8,64]{2,1,0:T(8,128)(2,1)} %weight_hbm.1, ...), custom_call_target="tpu_custom_call" | custom-call | tf_op jit(solution)/shard_map/pallas_call | solution.py:419
  22.3 0.6 %shard_map.96 = (f32[8,1600]{1,0:T(8,128)}, f32[8,40]{1,0:T(8,128)}) custom-call(f32[8,1600]{1,0:T(8,128)S(1)} %get-tuple-element.4.normal_in, f32[8,40]{1,0:T(8,128)S(1)} %get-tuple-element.5.grad_in), custom_call_target="tpu_custom_call" | custom-call | tf_op jit(solution)/shard_map/pallas_call | solution.py:453
